TPU v7x, 32 devices: a whole 2x2x4 slice. The times are simulated.
32 devices in a mesh: dp: 4 (over y, x), expert: 8 (over z, core).
Axes of the slice: x: 2, y: 2, z: 4, core: 2. Of those that a mesh axis runs over, the one named last changes fastest.
Arguments:
- features: bfloat16 [8192, 512], P(('dp', 'expert')), may hold values from -6 to 6
- slots: int32 [8192], P(('dp', 'expert')), may hold values from 0 to 31
- routes: int32 [8192, 2], P(('dp', 'expert')), may hold values from 0 to 7, all different within a row; in each aligned block of 256 rows (0 to 255, 256 to 511, ...) at most 128 rows name the same one
- cotangent: bfloat16 [8192, 512], P(('dp', 'expert')), may hold values from -1.5 to 1.5
- pos_table: bfloat16 [32, 64], replicated, may hold values from -6 to 6
- tower_in: bfloat16 [64, 256], replicated, may hold values from -0.75 to 0.75
- tower_out: bfloat16 [256, 512], replicated, may hold values from -0.375 to 0.375
- router: bfloat16 [512, 8], replicated, may hold values from -0.5 to 0.5
- w_up: bfloat16 [8, 512, 2048], P('expert'), may hold values from -0.25 to 0.25
- w_down: bfloat16 [8, 2048, 512], P('expert'), may hold values from -0.125 to 0.125
Outputs:
- layer_out: bfloat16 [8192, 512], P(('dp', 'expert'))
- grad_in: bfloat16 [8192, 512], P(('dp', 'expert'))
- grad_up: bfloat16 [8, 512, 2048], P('expert')
- grad_down: bfloat16 [8, 2048, 512], P('expert')
Inputs may be any that keep to these rules, and one draw needn't show every extreme that they name: `routes`: within the rows of one device no expert is named by more than 128 rows; in some devices' rows one expert is named by exactly 128.
All inputs are finite; a program needn't handle non-finite values.
Results may differ from a plain program's by a relative error of at most 0.013.
Values may be sent and summed in bfloat16 or wider, within the bound.
A program may use at most 128 MiB of HBM per device.

v0:
```python
import jax
import jax.numpy as jnp
from jax import lax
from jax.sharding import PartitionSpec as P

TOP = 2


coef_a = 0.7978845608028654
coef_b = 0.044715


def gelu_pair(pre_act):
    inner = coef_a * (pre_act + coef_b * pre_act * pre_act * pre_act)
    tanh_val = jnp.tanh(inner)
    activated = 0.5 * pre_act * (1.0 + tanh_val)
    gelu_slope = 0.5 * (1.0 + tanh_val) + 0.5 * pre_act * (1.0 - tanh_val * tanh_val) * coef_a * (
        1.0 + 3.0 * coef_b * pre_act * pre_act
    )
    return (activated, gelu_slope)


def contract_rows(left, right):
    return lax.dot_general(
        left, right, (((0,), (0,)), ((), ())), preferred_element_type=jnp.float32
    )


def contract_cols(left, right):
    return lax.dot_general(
        left, right, (((1,), (1,)), ((), ())), preferred_element_type=jnp.float32
    )


def expert_forward(flat_in, w_up_one, w_down_one):
    pre_act = jnp.dot(flat_in, w_up_one, preferred_element_type=jnp.float32)
    activated, gelu_slope = gelu_pair(pre_act)
    hidden = activated.astype(jnp.bfloat16)
    outputs = jnp.dot(hidden, w_down_one, preferred_element_type=jnp.float32).astype(jnp.bfloat16)
    return (hidden, gelu_slope, outputs)


def expert_backward(flat_in, flat_cot, hidden, gelu_slope, w_up_one, w_down_one):
    grad_down_part = contract_rows(hidden, flat_cot)
    d_hidden = contract_cols(flat_cot, w_down_one)
    d_pre = (d_hidden * gelu_slope).astype(jnp.bfloat16)
    d_inputs = contract_cols(d_pre, w_up_one).astype(jnp.bfloat16)
    grad_up_part = contract_rows(flat_in, d_pre)
    sum_up, sum_down = (
        lax.psum(grad_up_part.astype(jnp.bfloat16), "dp").astype(jnp.float32),
        lax.psum(grad_down_part.astype(jnp.bfloat16), "dp").astype(jnp.float32),
    )
    return (d_inputs, sum_up, sum_down)


def per_device(
    features, slots, routes, cotangent, pos_table, tower_in, tower_out, router, w_up, w_down
):
    tok_rows = features.shape[0]
    feature_width = features.shape[1]
    n_experts = router.shape[1]
    capacity = 2 * TOP * tok_rows // n_experts
    pos_hidden = jax.nn.relu(jnp.dot(pos_table, tower_in, preferred_element_type=jnp.float32))
    pos_rows = jnp.dot(pos_hidden, tower_out.astype(jnp.float32), precision=lax.Precision.HIGHEST)
    slot_hot = (slots[:, None] == jnp.arange(pos_table.shape[0], dtype=jnp.int32)[None, :]).astype(
        jnp.float32
    )
    pos_feats = jnp.dot(slot_hot, pos_rows, precision=lax.Precision.HIGHEST)
    mixed_in = (features.astype(jnp.float32) + pos_feats).astype(jnp.bfloat16)
    logits = jnp.dot(mixed_in, router, preferred_element_type=jnp.float32)
    expert_ids = jnp.arange(n_experts, dtype=jnp.int32)
    route_hot = routes[:, :, None] == expert_ids[None, None, :]
    chosen = jnp.sum(jnp.where(route_hot, logits[:, None, :], 0.0), axis=2)
    squashed = 1.0 / (1.0 + jnp.exp(-chosen))
    gate_total = jnp.sum(squashed, axis=1, keepdims=True)
    gates = squashed / gate_total
    cot_wide = cotangent.astype(jnp.float32)
    slot_cot = (gates[:, :, None] * cot_wide[:, None, :]).astype(jnp.bfloat16)
    flat_routes = routes.reshape(-1)
    flat_hot = route_hot.reshape(-1, n_experts).astype(jnp.int32)
    before = jnp.cumsum(flat_hot, axis=0, dtype=jnp.int32) - flat_hot
    slot_rank = jnp.sum(before * flat_hot, axis=1, dtype=jnp.int32)
    slot_place = flat_routes * capacity + slot_rank
    buffer_shape = (n_experts, capacity, feature_width)
    send_in = (
        jnp.zeros((n_experts * capacity, feature_width), jnp.bfloat16)
        .at[slot_place]
        .set(jnp.repeat(mixed_in, TOP, axis=0))
        .reshape(buffer_shape)
    )
    send_cot = (
        jnp.zeros((n_experts * capacity, feature_width), jnp.bfloat16)
        .at[slot_place]
        .set(slot_cot.reshape(-1, feature_width))
        .reshape(buffer_shape)
    )
    w_up_one = w_up[0]
    w_down_one = w_down[0]
    recv_in = lax.all_to_all(send_in, "expert", split_axis=0, concat_axis=0, tiled=True)
    flat_in = recv_in.reshape(-1, feature_width)
    hidden, gelu_slope, outputs = expert_forward(flat_in, w_up_one, w_down_one)
    back_out = lax.all_to_all(
        outputs.reshape(buffer_shape), "expert", split_axis=0, concat_axis=0, tiled=True
    )
    recv_cot = lax.all_to_all(send_cot, "expert", split_axis=0, concat_axis=0, tiled=True)
    flat_cot = recv_cot.reshape(-1, feature_width)
    d_inputs, sum_up, sum_down = expert_backward(
        flat_in, flat_cot, hidden, gelu_slope, w_up_one, w_down_one
    )
    back_grad = lax.all_to_all(
        d_inputs.reshape(buffer_shape), "expert", split_axis=0, concat_axis=0, tiled=True
    )
    expert_out = back_out.reshape(-1, feature_width)[slot_place].reshape(
        tok_rows, TOP, feature_width
    )
    slot_grad = back_grad.reshape(-1, feature_width)[slot_place].reshape(
        tok_rows, TOP, feature_width
    )
    expert_wide = expert_out.astype(jnp.float32)
    layer_out = (
        mixed_in.astype(jnp.float32) + jnp.sum(gates[:, :, None] * expert_wide, axis=1)
    ).astype(jnp.bfloat16)
    d_gates = jnp.sum(expert_wide * cot_wide[:, None, :], axis=2)
    mean_term = jnp.sum(gates * d_gates, axis=1, keepdims=True)
    d_chosen = (d_gates - mean_term) / gate_total * squashed * (1.0 - squashed)
    d_logits = jnp.sum(jnp.where(route_hot, d_chosen[:, :, None], 0.0), axis=1)
    d_router = lax.dot_general(
        d_logits,
        router.astype(jnp.float32),
        (((1,), (1,)), ((), ())),
        precision=lax.Precision.HIGHEST,
    )
    grad_in = (cot_wide + jnp.sum(slot_grad.astype(jnp.float32), axis=1) + d_router).astype(
        jnp.bfloat16
    )
    return (
        layer_out,
        grad_in,
        sum_up.astype(jnp.bfloat16)[None],
        sum_down.astype(jnp.bfloat16)[None],
    )


def solution(mesh):
    return jax.shard_map(
        per_device,
        mesh=mesh,
        in_specs=(
            P(("dp", "expert"), None),
            P(("dp", "expert")),
            P(("dp", "expert"), None),
            P(("dp", "expert"), None),
            P(),
            P(),
            P(),
            P(),
            P("expert", None, None),
            P("expert", None, None),
        ),
        out_specs=(
            P(("dp", "expert"), None),
            P(("dp", "expert"), None),
            P("expert", None, None),
            P("expert", None, None),
        ),
        check_vma=False,
    )
```

profile of v0, /device:TPU:13, one launch (start us, length us, event | category | flops | bytes accessed | tf_op | source)
XLA Modules:
  0.0 224.7 jit_solution(6666221709939206003)
XLA Ops:
  7.2 0.8 broadcast_multiply_fusion
  8.0 0.8 copy.28
  9.4 1.1 reduce-window.6
  10.6 0.2 slice_reduce_fusion
  10.8 0.9 convolution_maximum_fusion
  11.7 1.2 fusion.35
  12.9 1.4 fusion.22
  14.3 0.3 broadcast_in_dim.26
  14.6 0.2 reshape.212
  14.9 3.5 %scatter_custom_fusion = bf16[1024,512]{1,0:T(8,128)(2,1)} fusion(s32[512]{0:T(512)S(1)} %bitcast.58, bf16[512,512]{1,0:T(8,128)(2,1)S(1)} %reshape.212, bf16[]{:T(256)} %constant.12.clone.1), kind=kCustom, calls=%fused_computation.39 | custom fusion | bytes 1048578 | tf_op jit(solution)/shard_map/scatter | solution.py:88
  18.4 5.6 %all-to-all-start = ((bf16[8,128,512]{2,1,0:T(8,128)(2,1)}), bf16[8,128,512]{2,1,0:T(8,128)(2,1)}, u32[]{:S(2)}, u32[]{:S(2)}) async-start(bf16[8,128,512]{2,1,0:T(8,128)(2,1)} %bitcast.4), calls=%async_computation | async-start | bytes 2097152 | tf_op jit(solution)/shard_map/all_to_all | solution.py:99
  24.0 0.9 fusion.36
  24.9 0.7 select_reduce_fusion.1
  25.6 0.6 fusion.34
  26.2 0.6 copy-done.3
  27.1 1.2 mul.133
  28.3 1.7 mul.134
  30.0 4.2 %scatter_custom_fusion.1 = bf16[1024,512]{1,0:T(8,128)(2,1)} fusion(s32[512]{0:T(512)S(1)} %bitcast.59, f32[512,512]{1,0:T(8,128)} %mul.134, f32[512]{0:T(512)S(1)} %reshape.190, bf16[]{:T(256)} %constant.12.clone.1), kind=kCustom, calls=%fused_computation.35 | custom fusion | flops 524288 | bytes 2099202 | tf_op jit(solution)/shard_map/scatter | solution.py:94
  34.2 12.8 %all-to-all-done = bf16[8,128,512]{2,1,0:T(8,128)(2,1)} async-done(((bf16[8,128,512]{2,1,0:T(8,128)(2,1)}), bf16[8,128,512]{2,1,0:T(8,128)(2,1)}, u32[]{:S(2)}, u32[]{:S(2)}) %all-to-all-start) | async-done | bytes 1048608 | tf_op jit(solution)/shard_map/all_to_all | solution.py:99
  47.0 7.1 %all-to-all-start.2 = ((bf16[8,128,512]{2,1,0:T(8,128)(2,1)}), bf16[8,128,512]{2,1,0:T(8,128)(2,1)S(1)}, u32[]{:S(2)}, u32[]{:S(2)}) async-start(bf16[8,128,512]{2,1,0:T(8,128)(2,1)} %bitcast.10), calls=%async_computation.2 | async-start | bytes 2097152 | tf_op jit(solution)/shard_map/all_to_all | solution.py:105
  54.2 4.3 %fusion.14 = f32[1024,2048]{1,0:T(8,128)S(1)} fusion(bf16[1024,512]{1,0:T(8,128)(2,1)} %bitcast.5, bf16[1,512,2048]{2,1,0:T(8,128)(2,1)} %param.18), kind=kOutput, calls=%fused_computation.23 | convolution fusion | flops 2147483648 | bytes 11534336 | tf_op jit(solution)/shard_map/dot_general | solution.py:36
  58.5 3.2 %copy-done.4 = f32[1024,2048]{1,0:T(8,128)} copy-done((f32[1024,2048]{1,0:T(8,128)}, f32[1024,2048]{1,0:T(8,128)S(1)}, u32[]{:S(2)}) %copy-start.4) | copy-done | bytes 8388632
  61.7 3.9 %fusion.19 = bf16[1024,512]{1,0:T(8,128)(2,1)} fusion(bf16[1,2048,512]{2,1,0:T(8,128)(2,1)S(1)} %copy-done, f32[1024,2048]{1,0:T(8,128)S(1)} %fusion.14), kind=kOutput, calls=%fused_computation.26 | convolution fusion | flops 2166882304 | bytes 11534336 | tf_op jit(solution)/shard_map/dot_general | solution.py:39
  65.6 11.6 %all-to-all-done.2 = bf16[8,128,512]{2,1,0:T(8,128)(2,1)S(1)} async-done(((bf16[8,128,512]{2,1,0:T(8,128)(2,1)}), bf16[8,128,512]{2,1,0:T(8,128)(2,1)S(1)}, u32[]{:S(2)}, u32[]{:S(2)}) %all-to-all-start.2) | async-done | bytes 1048608 | tf_op jit(solution)/shard_map/all_to_all | solution.py:105
  77.2 8.5 %fusion.8 = bf16[1,2048,512]{2,1,0:T(8,128)(2,1)} fusion(bf16[1024,512]{1,0:T(8,128)(2,1)S(1)} %bitcast.56, f32[1024,2048]{1,0:T(8,128)} %copy-done.4), kind=kOutput, calls=%fused_computation.17 | convolution fusion | flops 2167406592 | bytes 11534336 | tf_op jit(solution)/shard_map/dot_general | solution.py:24
  85.7 7.9 %fusion.6 = bf16[1024,2048]{1,0:T(8,128)(2,1)} fusion(f32[1024,2048]{1,0:T(8,128)S(1)} %copy-done.5, bf16[1024,512]{1,0:T(8,128)(2,1)S(1)} %bitcast.57, bf16[1,2048,512]{2,1,0:T(8,128)(2,1)S(1)} %copy-done), kind=kOutput, calls=%fused_computation.12 | convolution fusion | flops 2187329536 | bytes 15728640 | tf_op jit(solution)/shard_map/dot_general | solution.py:30
  93.6 7.0 %all-to-all-start.1 = ((bf16[8,128,512]{2,1,0:T(8,128)(2,1)}), bf16[8,128,512]{2,1,0:T(8,128)(2,1)S(1)}, u32[]{:S(2)}, u32[]{:S(2)}) async-start(bf16[8,128,512]{2,1,0:T(8,128)(2,1)} %bitcast.54), calls=%async_computation.1 | async-start | bytes 2097152 | tf_op jit(solution)/shard_map/all_to_all | solution.py:102
  100.7 6.2 %fusion.7 = bf16[1,512,2048]{2,1,0:T(8,128)(2,1)} fusion(bf16[1024,512]{1,0:T(8,128)(2,1)} %bitcast.5, bf16[1024,2048]{1,0:T(8,128)(2,1)} %fusion.6), kind=kOutput, calls=%fused_computation.16 | convolution fusion | flops 2148532224 | bytes 7340032 | tf_op jit(solution)/shard_map/dot_general | solution.py:24
  106.9 6.3 %fusion.16 = bf16[1024,512]{1,0:T(8,128)(2,1)} fusion(bf16[1024,2048]{1,0:T(8,128)(2,1)} %fusion.6, bf16[1,512,2048]{2,1,0:T(8,128)(2,1)} %param.18), kind=kOutput, calls=%fused_computation.25 | convolution fusion | flops 2148007936 | bytes 7340032 | tf_op jit(solution)/shard_map/dot_general | solution.py:30
  113.2 10.5 %all-to-all-done.1 = bf16[8,128,512]{2,1,0:T(8,128)(2,1)S(1)} async-done(((bf16[8,128,512]{2,1,0:T(8,128)(2,1)}), bf16[8,128,512]{2,1,0:T(8,128)(2,1)S(1)}, u32[]{:S(2)}, u32[]{:S(2)}) %all-to-all-start.1) | async-done | bytes 1048608 | tf_op jit(solution)/shard_map/all_to_all | solution.py:102
  123.7 7.9 %all-to-all-start.3 = ((bf16[8,128,512]{2,1,0:T(8,128)(2,1)}), bf16[8,128,512]{2,1,0:T(8,128)(2,1)}, u32[]{:S(2)}, u32[]{:S(2)}) async-start(bf16[8,128,512]{2,1,0:T(8,128)(2,1)} %bitcast.55), calls=%async_computation.3 | async-start | bytes 2097152 | tf_op jit(solution)/shard_map/all_to_all | solution.py:110
  131.6 1.8 convert_element_type.80
  133.4 0.6 pad_clamp_fusion
  134.0 2.9 %gather_fusion = bf16[512,512]{1,0:T(8,128)(2,1)} fusion(bf16[1024,512]{1,0:T(8,128)(2,1)S(1)} %bitcast.53, s32[1024]{0:T(1024)} %pad_clamp_fusion), kind=kCustom, calls=%fused_computation | custom fusion | bytes 1050624 | tf_op jit(solution)/shard_map/gather | solution.py:113
  136.9 1.7 reshape.188
  138.6 4.0 %multiply_reduce_fusion = (f32[256,2]{1,0:T(8,128)}, f32[256,512]{1,0:T(8,128)}) fusion(f32[256,2,512]{2,1,0:T(2,128)S(1)} %reshape.188, f32[256,512]{1,0:T(8,128)} %convert_element_type.80, f32[256,2]{1,0:T(8,128)S(1)} %copy.26), kind=kLoop, calls=%fused_computation.32 | loop fusion | flops 916992 | bytes 2101248 | tf_op jit(solution)/shard_map/reduce_sum | solution.py:123
  142.6 1.0 copy.32
  143.6 11.1 %all-to-all-done.3 = bf16[8,128,512]{2,1,0:T(8,128)(2,1)} async-done(((bf16[8,128,512]{2,1,0:T(8,128)(2,1)}), bf16[8,128,512]{2,1,0:T(8,128)(2,1)}, u32[]{:S(2)}, u32[]{:S(2)}) %all-to-all-start.3) | async-done | bytes 1048608 | tf_op jit(solution)/shard_map/all_to_all | solution.py:110
  154.6 4.2 %gather_fusion.1 = bf16[512,512]{1,0:T(8,128)(2,1)} fusion(bf16[1024,512]{1,0:T(8,128)(2,1)} %bitcast.13, s32[1024]{0:T(1024)} %pad_clamp_fusion), kind=kCustom, calls=%fused_computation.1 | custom fusion | bytes 1050624 | tf_op jit(solution)/shard_map/gather | solution.py:116
  158.8 1.7 reshape.191
  160.5 2.1 reduce_sum.79
  162.6 0.7 multiply_reduce_fusion.2
  163.3 0.7 fusion.33
  164.1 1.8 add_convert_fusion
  165.9 2.3 %fusion.23 = bf16[256,512]{1,0:T(8,128)(2,1)} fusion(f32[256,8]{0,1:T(8,128)S(1)} %select_reduce_fusion, bf16[512,8]{0,1:T(8,128)(2,1)S(1)} %copy-done.1, f32[256,512]{1,0:T(8,128)} %reduce_sum.79, bf16[256,512]{1,0:T(8,128)(2,1)} %param.13), kind=kOutput, calls=%fused_computation.30 | convolution fusion | flops 13107200 | bytes 1064960 | tf_op jit(solution)/shard_map/dot_general | solution.py:127
  168.2 43.5 %all-reduce.3.cloned.1.call-done = (bf16[1,512,2048]{2,1,0:T(8,128)(2,1)}, bf16[1,2048,512]{2,1,0:T(8,128)(2,1)}) async-done(((bf16[1,512,2048]{2,1,0:T(8,128)(2,1)}, bf16[1,2048,512]{2,1,0:T(8,128)(2,1)}), (bf16[1,512,2048]{2,1,0:T(8,128)(2,1)}, bf16[1,2048,512]{2,1,0:T(8,128)(2,1)})) %all-reduce.3.cloned.1.call-update) | async-done | bytes 4194320 | tf_op jit(solution)/shard_map/psum | solution.py:50
  211.6 3.2 %copy.35 = bf16[1,512,2048]{2,1,0:T(8,128)(2,1)} copy(bf16[1,512,2048]{2,1,0:T(8,128)(2,1)} %get-tuple-element.12) | data formatting | bytes 4194304
  214.8 3.0 %copy.36 = bf16[1,2048,512]{2,1,0:T(8,128)(2,1)} copy(bf16[1,2048,512]{2,1,0:T(8,128)(2,1)} %get-tuple-element.13) | data formatting | bytes 4194304
  (25 shorter events, 1.1 us)
Async XLA Ops:
  7.2 54.5 %copy-start = (bf16[1,2048,512]{2,1,0:T(8,128)(2,1)S(1)}, bf16[1,2048,512]{2,1,0:T(8,128)(2,1)}, u32[]{:S(2)}) copy-start(bf16[1,2048,512]{2,1,0:T(8,128)(2,1)} %param.19) | copy-start | bytes 6291460
  18.4 28.7 %all-to-all-start = ((bf16[8,128,512]{2,1,0:T(8,128)(2,1)}), bf16[8,128,512]{2,1,0:T(8,128)(2,1)}, u32[]{:S(2)}, u32[]{:S(2)}) async-start(bf16[8,128,512]{2,1,0:T(8,128)(2,1)} %bitcast.4), calls=%async_computation | async-start | bytes 2097152 | tf_op jit(solution)/shard_map/all_to_all | solution.py:99
  26.2 0.6 copy-start.3
  47.0 30.2 %all-to-all-start.2 = ((bf16[8,128,512]{2,1,0:T(8,128)(2,1)}), bf16[8,128,512]{2,1,0:T(8,128)(2,1)S(1)}, u32[]{:S(2)}, u32[]{:S(2)}) async-start(bf16[8,128,512]{2,1,0:T(8,128)(2,1)} %bitcast.10), calls=%async_computation.2 | async-start | bytes 2097152 | tf_op jit(solution)/shard_map/all_to_all | solution.py:105
  58.4 3.2 %copy-start.4 = (f32[1024,2048]{1,0:T(8,128)}, f32[1024,2048]{1,0:T(8,128)S(1)}, u32[]{:S(2)}) copy-start(f32[1024,2048]{1,0:T(8,128)S(1)} %fusion.14) | copy-start | bytes 25165828
  77.2 8.5 %copy-start.5 = (f32[1024,2048]{1,0:T(8,128)S(1)}, f32[1024,2048]{1,0:T(8,128)}, u32[]{:S(2)}) copy-start(f32[1024,2048]{1,0:T(8,128)} %copy-done.4) | copy-start | bytes 25165828
  93.6 30.1 %all-to-all-start.1 = ((bf16[8,128,512]{2,1,0:T(8,128)(2,1)}), bf16[8,128,512]{2,1,0:T(8,128)(2,1)S(1)}, u32[]{:S(2)}, u32[]{:S(2)}) async-start(bf16[8,128,512]{2,1,0:T(8,128)(2,1)} %bitcast.54), calls=%async_computation.1 | async-start | bytes 2097152 | tf_op jit(solution)/shard_map/all_to_all | solution.py:102
  100.7 111.0 %all-reduce.3.cloned.1.call-start = ((), (), s32[]{:S(2)}) async-start(), calls=%async_computation.4 | async-start | bytes 8388608 | tf_op jit(solution)/shard_map/psum | solution.py:50
  123.7 30.9 %all-to-all-start.3 = ((bf16[8,128,512]{2,1,0:T(8,128)(2,1)}), bf16[8,128,512]{2,1,0:T(8,128)(2,1)}, u32[]{:S(2)}, u32[]{:S(2)}) async-start(bf16[8,128,512]{2,1,0:T(8,128)(2,1)} %bitcast.55), calls=%async_computation.3 | async-start | bytes 2097152 | tf_op jit(solution)/shard_map/all_to_all | solution.py:110
  133.4 30.6 %copy-start.2 = (s32[256,2]{0,1:T(2,128)S(1)}, s32[256,2]{0,1:T(2,128)}, u32[]{:S(2)}) copy-start(s32[256,2]{0,1:T(2,128)} %param.12) | copy-start | bytes 6148
  134.0 31.9 %copy-start.1 = (bf16[512,8]{0,1:T(8,128)(2,1)S(1)}, bf16[512,8]{0,1:T(8,128)(2,1)}, u32[]{:S(2)}) copy-start(bf16[512,8]{0,1:T(8,128)(2,1)} %param.17) | copy-start | bytes 24580
Sparse Core Ops, SparseCore 0:
  107.0 104.6 all-reduce.2
where the time goes:
time: 228 us; the launch traced here: 225 us
  waiting for transfers between devices  89.5 us (39%)
  matrix products  43.7 us (19%)
  local copies, waits for them, and re-layouts  30.2 us (13%)
  starting transfers between devices  27.7 us (12%)
  other arithmetic  19.4 us (9%)
  between operations  14.2 us (6%)
    psum x1, waiting for transfers between devices, expert_backward(): lax.psum(grad_up_part.astype(jnp.bfloat16), 'dp').astype(jnp.float32)  43.5 us
    dot_general x2, matrix products, contract_rows(): lax.dot_general(left, right, (((0,), (0,)), ((), ())), preferred_element_...  14.7 us
    dot_general x2, matrix products, contract_cols(): lax.dot_general(left, right, (((1,), (1,)), ((), ())), preferred_element_...  14.2 us
    all_to_all x1, waiting for transfers between devices, per_device(): lax.all_to_all(send_in, 'expert', split_axis=0, concat_axis=0, tiled=True)  12.8 us
    all_to_all x1, waiting for transfers between devices, per_device(): lax.all_to_all(send_cot, 'expert', split_axis=0, concat_axis=0, tiled=True)  11.6 us
    all_to_all x1, waiting for transfers between devices, per_device(): lax.all_to_all(d_inputs.reshape(buffer_shape), 'expert', split_axis=0, co...  11.1 us
    unnamed x15, local copies, waits for them, and re-layouts  10.8 us
    all_to_all x1, waiting for transfers between devices, per_device(): lax.all_to_all(outputs.reshape(buffer_shape), 'expert', split_axis=0, con...  10.5 us
  transfers between devices with their start and end apart: 5, of which 5 were waited for; matrix products, arithmetic and copies ran while one was open for 25% of the time, Pallas kernels for 0%

commit v1 on v0

v1 whole, which is shorter than its diff:
```python
import functools

import jax
import jax.numpy as jnp
from jax import lax
from jax.experimental import pallas as pl
from jax.experimental.pallas import tpu as pltpu
from jax.sharding import PartitionSpec as P

coef_a = 0.7978845608028654
coef_b = 0.044715
MESH = pl.DeviceIdType.MESH
F32, BF16 = jnp.float32, jnp.bfloat16
EXACT = lax.Precision.HIGHEST


def gelu_pair(pre_act):
    square = pre_act * pre_act
    tanh_val = jnp.tanh(coef_a * pre_act * (1.0 + coef_b * square))
    half = 0.5 * (1.0 + tanh_val)
    slope = half + 0.5 * pre_act * (1.0 - tanh_val * tanh_val) * (
        coef_a * (1.0 + 3.0 * coef_b * square)
    )
    return pre_act * half, slope


def dot(left, right, dims, precision=None):
    return lax.dot_general(
        left, right, ((dims[:1], dims[1:]), ((), ())),
        precision=precision, preferred_element_type=F32,
    )


def kernel(
    sizes,
    features, slots, routes, cotangent, pos_table, tower_in, tower_out, router, w_up, w_down,
    layer_out, grad_in, grad_up, grad_down,
    mixed_s, place_s, gate_s, squash_s,
    send_in, send_cot, recv_in, recv_cot, hid, slope, outs, d_acc, d_ins, back_out, back_grad,
    part_up, part_down, one_up, one_down, two_up, two_down,
    ex_send, ex_recv, ar_send, ar_recv,
):
    n_exp, cap, tiles = sizes
    tok, width = features.shape
    hidden = w_up.shape[1]
    step = hidden // tiles
    dp, me = lax.axis_index("dp"), lax.axis_index("expert")
    xb, yb = dp % 2, dp // 2
    x_peer, y_peer = dp + 1 - 2 * xb, dp + 2 - 4 * yb

    barrier = pltpu.get_barrier_semaphore()

    @pl.loop(1, n_exp)
    def _(d):
        pl.semaphore_signal(barrier, inc=1, device_id=(dp, (me + d) % n_exp), device_id_type=MESH)

    for peer in (x_peer, y_peer):
        pl.semaphore_signal(barrier, inc=1, device_id=(peer, me), device_id_type=MESH)

    pos_hidden = jnp.maximum(dot(pos_table[...], tower_in[...], (1, 0)), 0.0)
    pos_rows = dot(pos_hidden, tower_out[...].astype(F32), (1, 0), EXACT)
    n_pos = pos_table.shape[0]
    slot_hot = (slots[...] == lax.broadcasted_iota(jnp.int32, (tok, n_pos), 1)).astype(F32)
    pos_feats = dot(slot_hot, pos_rows, (1, 0), EXACT)
    mixed = (features[...].astype(F32) + pos_feats).astype(BF16)
    mixed_s[...] = mixed
    logits = dot(mixed, router[...], (1, 0))
    expert_ids = lax.broadcasted_iota(jnp.int32, (tok, n_exp), 1)
    hots = [(routes[:, k : k + 1] == expert_ids).astype(F32) for k in range(2)]
    earlier = (
        lax.broadcasted_iota(jnp.int32, (tok, tok), 1)
        < lax.broadcasted_iota(jnp.int32, (tok, tok), 0)
    ).astype(F32)
    before = dot(earlier.astype(BF16), (hots[0] + hots[1]).astype(BF16), (1, 0))
    squashed = [
        1.0 / (1.0 + jnp.exp(-jnp.sum(hot * logits, axis=1, keepdims=True))) for hot in hots
    ]
    total = squashed[0] + squashed[1]
    gates = [s / total for s in squashed]
    cot_wide = cotangent[...].astype(F32)
    cells = lax.broadcasted_iota(jnp.int32, (tok, n_exp * cap), 1)
    picks = []
    for k in range(2):
        rank = jnp.sum(hots[k] * before, axis=1, keepdims=True).astype(jnp.int32)
        place = routes[:, k : k + 1] * cap + rank
        place_s[:, k : k + 1] = place
        gate_s[:, k : k + 1] = gates[k]
        squash_s[:, k : k + 1] = squashed[k]
        picks.append((place == cells).astype(F32).astype(BF16))
    send_in[...] = dot(picks[0] + picks[1], mixed, (0, 0)).astype(BF16)

    pl.semaphore_wait(barrier, n_exp + 1)

    def exchange(number, source, target, d):
        peer = (me + d) % n_exp
        return pltpu.make_async_remote_copy(
            src_ref=source.at[pl.ds(pl.multiple_of(peer * cap, cap), cap)],
            dst_ref=target.at[pl.ds(pl.multiple_of(me * cap, cap), cap)],
            send_sem=ex_send.at[number, d],
            recv_sem=ex_recv.at[number, d],
            device_id=(dp, peer),
            device_id_type=MESH,
        )

    def start_exchange(number, source, target):
        @pl.loop(1, n_exp)
        def _(d):
            exchange(number, source, target, d).start()

        own = pl.ds(pl.multiple_of(me * cap, cap), cap)
        target[own, :] = source[own, :]

    def arrived(number, target):
        @pl.loop(1, n_exp)
        def _(d):
            giver = (me - d + n_exp) % n_exp
            rows = pl.ds(pl.multiple_of(giver * cap, cap), cap)
            pltpu.make_async_remote_copy(
                src_ref=target.at[rows],
                dst_ref=target.at[rows],
                send_sem=ex_send.at[number, d],
                recv_sem=ex_recv.at[number, d],
                device_id=(dp, (me + d) % n_exp),
                device_id_type=MESH,
            ).wait_recv()

    def sent(number, source, target):
        @pl.loop(1, n_exp)
        def _(d):
            exchange(number, source, target, d).wait_send()

    start_exchange(0, send_in, recv_in)
    cots = [(g * cot_wide).astype(BF16) for g in gates]
    send_cot[...] = (dot(picks[0], cots[0], (0, 0)) + dot(picks[1], cots[1], (0, 0))).astype(BF16)
    start_exchange(1, send_cot, recv_cot)
    arrived(0, recv_in)

    @pl.loop(0, tiles)
    def _(t):
        cols = pl.ds(pl.multiple_of(t * step, step), step)
        act, der = gelu_pair(dot(recv_in[...], w_up[:, cols], (1, 0)))
        act = act.astype(BF16)
        hid[t] = act
        slope[t] = der
        term = dot(act, w_down[cols, :], (1, 0))

        @pl.when(t == 0)
        def _():
            d_acc[...] = term

        @pl.when(t > 0)
        def _():
            d_acc[...] += term

    outs[...] = d_acc[...].astype(BF16)
    arrived(1, recv_cot)
    start_exchange(2, outs, back_out)

    half_u, half_d = width // 2, step // 2
    quart_u, quart_d = width // 4, step // 4

    def rows_of(big, index, size, small=None, inner=0):
        at = big + index * size
        if small is not None:
            at = at + inner * small
        return pl.multiple_of(at, small or size)

    def reduce_copy(phase, which, t):
        cols = pl.ds(pl.multiple_of(t * step, step), step)
        if which == 0:
            a, b = xb, yb
            first, second = (x_peer, me), (y_peer, me)
            base, half, quart = 0, half_u, quart_u
            part, one, two, final = part_up, one_up, two_up, grad_up
        else:
            a, b = yb, xb
            first, second = (y_peer, me), (x_peer, me)
            base, half, quart = t * step, half_d, quart_d
            part, one, two, final = part_down, one_down, two_down, grad_down

        def view(ref, start, size):
            rows = pl.ds(start, size)
            return ref.at[rows, cols] if which == 0 else ref.at[rows]

        if phase == 0:
            src, dst, peer = view(part, rows_of(base, 1 - a, half), half), one.at[t], first
        elif phase == 1:
            src = view(part, rows_of(base, a, half, quart, 1 - b), quart)
            dst, peer = two.at[t], second
        elif phase == 2:
            src = dst = view(final, rows_of(base, a, half, quart, b), quart)
            peer = second
        else:
            src = dst = view(final, rows_of(base, a, half), half)
            peer = first
        return pltpu.make_async_remote_copy(
            src_ref=src, dst_ref=dst,
            send_sem=ar_send.at[phase, which, t], recv_sem=ar_recv.at[phase, which, t],
            device_id=peer, device_id_type=MESH,
        )

    @pl.loop(0, tiles)
    def _(t):
        cols = pl.ds(pl.multiple_of(t * step, step), step)
        d_hidden = dot(recv_cot[...], w_down[cols, :], (1, 1))
        part_down[cols, :] = dot(hid[t], recv_cot[...], (0, 0)).astype(BF16)
        reduce_copy(0, 1, t).start()
        d_pre = (d_hidden * slope[t]).astype(BF16)
        part_up[:, cols] = dot(recv_in[...], d_pre, (0, 0)).astype(BF16)
        reduce_copy(0, 0, t).start()
        term = dot(d_pre, w_up[:, cols], (1, 1))

        @pl.when(t == 0)
        def _():
            d_acc[...] = term

        @pl.when(t > 0)
        def _():
            d_acc[...] += term

    d_ins[...] = d_acc[...].astype(BF16)
    start_exchange(3, d_ins, back_grad)

    @pl.loop(0, tiles)
    def _(t):
        cols = pl.ds(pl.multiple_of(t * step, step), step)
        reduce_copy(0, 1, t).wait_recv()
        rows = pl.ds(rows_of(t * step, yb, half_d), half_d)
        part_down[rows, :] = (part_down[rows, :].astype(F32) + one_down[t].astype(F32)).astype(BF16)
        reduce_copy(1, 1, t).start()
        reduce_copy(0, 0, t).wait_recv()
        rows = pl.ds(rows_of(0, xb, half_u), half_u)
        part_up[rows, cols] = (part_up[rows, cols].astype(F32) + one_up[t].astype(F32)).astype(BF16)
        reduce_copy(1, 0, t).start()

    @pl.loop(0, tiles)
    def _(t):
        cols = pl.ds(pl.multiple_of(t * step, step), step)
        reduce_copy(1, 1, t).wait_recv()
        rows = pl.ds(rows_of(t * step, yb, half_d, quart_d, xb), quart_d)
        grad_down[rows, :] = (part_down[rows, :].astype(F32) + two_down[t].astype(F32)).astype(BF16)
        reduce_copy(2, 1, t).start()
        reduce_copy(1, 0, t).wait_recv()
        rows = pl.ds(rows_of(0, xb, half_u, quart_u, yb), quart_u)
        grad_up[rows, cols] = (part_up[rows, cols].astype(F32) + two_up[t].astype(F32)).astype(BF16)
        reduce_copy(2, 0, t).start()

    def gathered(phase, which, t):
        cols = pl.ds(pl.multiple_of(t * step, step), step)
        a, b = (xb, yb) if which == 0 else (yb, xb)
        base, half, quart = (0, half_u, quart_u) if which == 0 else (t * step, half_d, quart_d)
        if phase == 2:
            rows = pl.ds(rows_of(base, a, half, quart, 1 - b), quart)
        else:
            rows = pl.ds(rows_of(base, 1 - a, half), half)
        ref = grad_up.at[rows, cols] if which == 0 else grad_down.at[rows]
        pltpu.make_async_remote_copy(
            src_ref=ref, dst_ref=ref,
            send_sem=ar_send.at[phase, which, t], recv_sem=ar_recv.at[phase, which, t],
            device_id=(x_peer, me), device_id_type=MESH,
        ).wait_recv()

    @pl.loop(0, tiles)
    def _(t):
        for which in (1, 0):
            gathered(2, which, t)
            reduce_copy(3, which, t).start()

    arrived(2, back_out)
    arrived(3, back_grad)
    cells = lax.broadcasted_iota(jnp.int32, (tok, n_exp * cap), 1)
    picks = [(place_s[:, k : k + 1] == cells).astype(F32).astype(BF16) for k in range(2)]
    gates = [gate_s[:, k : k + 1] for k in range(2)]
    squashed = [squash_s[:, k : k + 1] for k in range(2)]
    total = squashed[0] + squashed[1]
    cot_wide = cotangent[...].astype(F32)
    expert_out = [dot(pick, back_out[...], (1, 0)) for pick in picks]
    layer_out[...] = (
        mixed_s[...].astype(F32) + (gates[0] * expert_out[0] + gates[1] * expert_out[1])
    ).astype(BF16)
    d_gates = [jnp.sum(o * cot_wide, axis=1, keepdims=True) for o in expert_out]
    mean_term = gates[0] * d_gates[0] + gates[1] * d_gates[1]
    expert_ids = lax.broadcasted_iota(jnp.int32, (tok, n_exp), 1)
    d_logits = jnp.zeros((tok, n_exp), F32)
    for k in range(2):
        d_chosen = (d_gates[k] - mean_term) / total * squashed[k] * (1.0 - squashed[k])
        d_logits += jnp.where(routes[:, k : k + 1] == expert_ids, d_chosen, 0.0)
    d_router = dot(d_logits, router[...].astype(F32), (1, 1), EXACT)
    slot_sum = dot(picks[0] + picks[1], back_grad[...], (1, 0))
    grad_in[...] = (cot_wide + slot_sum + d_router).astype(BF16)

    sent(0, send_in, recv_in)
    sent(1, send_cot, recv_cot)
    sent(2, outs, back_out)
    sent(3, d_ins, back_grad)

    @pl.loop(0, tiles)
    def _(t):
        for which in (1, 0):
            gathered(3, which, t)
            for phase in range(4):
                reduce_copy(phase, which, t).wait_send()


def per_device(
    features, slots, routes, cotangent, pos_table, tower_in, tower_out, router, w_up, w_down
):
    tok, width = features.shape
    n_exp = router.shape[1]
    hidden = w_up.shape[2]
    cap = 4 * tok // n_exp
    rows = n_exp * cap
    tiles = 8
    step = hidden // tiles
    vmem = pl.BlockSpec(memory_space=pltpu.VMEM)
    dma = pltpu.SemaphoreType.DMA
    outs = pl.pallas_call(
        functools.partial(kernel, (n_exp, cap, tiles)),
        out_shape=(
            jax.ShapeDtypeStruct((tok, width), BF16),
            jax.ShapeDtypeStruct((tok, width), BF16),
            jax.ShapeDtypeStruct((width, hidden), BF16),
            jax.ShapeDtypeStruct((hidden, width), BF16),
        ),
        in_specs=[vmem] * 10,
        out_specs=(vmem,) * 4,
        scratch_shapes=[
            pltpu.VMEM((tok, width), BF16),
            pltpu.VMEM((tok, 2), jnp.int32),
            pltpu.VMEM((tok, 2), F32),
            pltpu.VMEM((tok, 2), F32),
            pltpu.VMEM((rows, width), BF16),
            pltpu.VMEM((rows, width), BF16),
            pltpu.VMEM((rows, width), BF16),
            pltpu.VMEM((rows, width), BF16),
            pltpu.VMEM((tiles, rows, step), BF16),
            pltpu.VMEM((tiles, rows, step), F32),
            pltpu.VMEM((rows, width), BF16),
            pltpu.VMEM((rows, width), F32),
            pltpu.VMEM((rows, width), BF16),
            pltpu.VMEM((rows, width), BF16),
            pltpu.VMEM((rows, width), BF16),
            pltpu.VMEM((width, hidden), BF16),
            pltpu.VMEM((hidden, width), BF16),
            pltpu.VMEM((tiles, width // 2, step), BF16),
            pltpu.VMEM((tiles, step // 2, width), BF16),
            pltpu.VMEM((tiles, width // 4, step), BF16),
            pltpu.VMEM((tiles, step // 4, width), BF16),
            dma((4, n_exp)),
            dma((4, n_exp)),
            dma((4, 2, tiles)),
            dma((4, 2, tiles)),
        ],
        compiler_params=pltpu.CompilerParams(
            collective_id=0, has_side_effects=True, vmem_limit_bytes=60 * 1024 * 1024
        ),
    )(
        features, slots[:, None], routes, cotangent, pos_table, tower_in, tower_out, router,
        w_up[0], w_down[0],
    )
    return outs[0], outs[1], outs[2][None], outs[3][None]


def solution(mesh):
    return jax.shard_map(
        per_device,
        mesh=mesh,
        in_specs=(
            P(("dp", "expert"), None),
            P(("dp", "expert")),
            P(("dp", "expert"), None),
            P(("dp", "expert"), None),
            P(),
            P(),
            P(),
            P(),
            P("expert", None, None),
            P("expert", None, None),
        ),
        out_specs=(
            P(("dp", "expert"), None),
            P(("dp", "expert"), None),
            P("expert", None, None),
            P("expert", None, None),
        ),
        check_vma=False,
    )
```

time: 228 us -> 142 us (0.62); the launches traced: 225 us -> 141 us
  Pallas kernels: 0 us -> 128 us
  waiting for transfers between devices: 89.5 us -> 0 us
  matrix products: 43.7 us -> 0 us
  starting transfers between devices: 27.7 us -> 0 us
  other arithmetic: 19.4 us -> 0 us
  local copies, waits for them, and re-layouts: 30.2 us -> 12.4 us
  between operations: 14.2 us -> 0.64 us
    pallas_call x0 -> x1, Pallas kernels: none -> 128 us  [per_device(): pl.pallas_call(functools.partial(kernel, (n_exp, cap, tiles)), out_shape=...]
    all_to_all x4 -> x0, waiting for transfers between devices: 46 us -> none  [the longest x1 12.8 us: per_device(): lax.all_to_all(send_in, 'expert', split_axis=0, concat_axis=0, tiled=True)]
    dot_general x11 -> x0, matrix products: 43.7 us -> none  [the longest x2 14.7 us: contract_rows(): lax.dot_general(left, right, (((0,), (0,)), ((), ())), preferred_element_...]
    psum x1 -> x0, waiting for transfers between devices: 43.5 us -> none  [expert_backward(): lax.psum(grad_up_part.astype(jnp.bfloat16), 'dp').astype(jnp.float32)]
    all_to_all x4 -> x0, starting transfers between devices: 27.7 us -> none  [the longest x1 7.91 us: per_device(): lax.all_to_all(d_inputs.reshape(buffer_shape), 'expert', split_axis=0, co...]
    reduce_sum x7 -> x0, other arithmetic: 8.23 us -> none  [the longest x1 3.97 us: per_device(): d_gates = jnp.sum(expert_wide * cot_wide[:, None, :], axis=2)]
    gather x2 -> x0, local copies, waits for them, and re-layouts: 7.06 us -> none  [the longest x1 4.15 us: per_device(): back_grad.reshape(-1, feature_width)[slot_place]]
    scatter x1 -> x0, other arithmetic: 4.2 us -> none  [per_device(): send_cot = jnp.zeros((n_experts * capacity, feature_width), jnp.bfloat16)...]
  transfers between devices with their start and end apart: 5 -> 0, of which waited for: 5 -> 0; matrix products, arithmetic and copies ran while one was open for 25% -> 0% of each run, Pallas kernels for 0% -> 0%
where the time goes in v1:
time: 142 us; the launch traced here: 141 us
  Pallas kernels  128 us (90%)
  local copies, waits for them, and re-layouts  12.4 us (9%)
    pallas_call x1, Pallas kernels, per_device(): pl.pallas_call(functools.partial(kernel, (n_exp, cap, tiles)), out_shape=...  128 us
    unnamed x8, local copies, waits for them, and re-layouts  10.9 us

profile of v1, /device:TPU:13, one launch (start us, length us, event | category | flops | bytes accessed | tf_op | source)
XLA Modules:
  0.0 141.5 jit_solution(7897086480225063466)
XLA Ops:
  0.6 1.5 %copy.16.slots = s32[256,1]{1,0:T(8,128)} copy(s32[256,1]{0,1:T(1,128)} %bitcast.9) | data formatting | bytes 2048 | tf_op jit(solution)/shard_map/broadcast_in_dim | solution.py:358
  2.1 1.5 %copy.17.routes = s32[256,2]{1,0:T(8,128)} copy(s32[256,2]{0,1:T(2,128)} %param.12) | data formatting | bytes 4096 | tf_op args[2]
  3.6 1.5 %copy.18.router = bf16[512,8]{1,0:T(8,128)(2,1)} copy(bf16[512,8]{0,1:T(8,128)(2,1)} %param.17) | data formatting | bytes 16384 | tf_op args[7]
  5.1 128.4 %shard_map.129 = (bf16[256,512]{1,0:T(8,128)(2,1)}, bf16[256,512]{1,0:T(8,128)(2,1)}, bf16[512,2048]{1,0:T(8,128)(2,1)}, bf16[2048,512]{1,0:T(8,128)(2,1)}) custom-call(bf16[256,512]{1,0:T(8,128)(2,1)} %features.1, s32[256,1]{1,0:T(8,128)} %copy.16.slots, s32[256,2]{1,0:T(8,128)} %copy.17.routes, bf16[256,512]{1,0:T(8,128)(2,1)} %cotangent.1, ...), custom_call_target="tpu_custom_call" | custom-call | tf_op jit(solution)/shard_map/pallas_call | solution.py:317
  133.5 1.7 %copy.23 = bf16[256,512]{1,0:T(8,128)(2,1)} copy(bf16[256,512]{1,0:T(8,128)(2,1)} %get-tuple-element.16) | data formatting | bytes 524288
  135.2 1.7 %copy.24 = bf16[256,512]{1,0:T(8,128)(2,1)} copy(bf16[256,512]{1,0:T(8,128)(2,1)} %get-tuple-element.17) | data formatting | bytes 524288
  136.8 0.0 copy-start
  136.8 3.3 %copy.25 = bf16[1,512,2048]{2,1,0:T(8,128)(2,1)} copy(bf16[1,512,2048]{2,1,0:T(8,128)(2,1)} %bitcast.8) | data formatting | bytes 4194304
  140.1 0.0 copy-done
  140.1 1.3 copy.26
Async XLA Ops:
  136.8 3.3 %copy-start = (bf16[2048,512]{1,0:T(8,128)(2,1)S(1)}, bf16[2048,512]{1,0:T(8,128)(2,1)}, u32[]{:S(2)}) copy-start(bf16[2048,512]{1,0:T(8,128)(2,1)} %get-tuple-element.11) | copy-start | bytes 6291460
